TPU v7x, 128 devices: a whole 4x4x4 slice. The times are simulated.
128 devices in a mesh: depth: 2 (over core), rows: 2 (over x_hi), shots: 32 (over z, y, x_lo).
Axes of the slice: x: 4 (x_hi: 2, x_lo: 2; x = x_hi * 2 + x_lo), y: 4, z: 4, core: 2. Of those that a mesh axis runs over, the one named last changes fastest.
Arguments:
- sources: float32 [2, 2, 1024, 4096], P('depth', None, 'rows', 'shots'), may hold values from -6 to 6
- factor: float32 [2, 2, 1024, 1024], P('depth', None, ('rows', 'shots')), may hold values from -0.09375 to 0.09375
- block_mask: int32 [2, 2, 8, 8], P('depth'), may hold values 0 or 1
- inverse_diagonal: float32 [2, 2, 1024, 1024], P('depth', None, None, 'rows'), may hold values from -1.2 to 1.2, as said below
Outputs:
- solution: float32 [2, 2, 1024, 4096], P('depth', None, 'rows', 'shots')
Inputs may be any that keep to these rules, and one draw needn't show every extreme that they name: Each block inverse_diagonal[d, m] is lower triangular with diagonal entries between 0.8 and 1.2.
All inputs are finite; a program needn't handle non-finite values. No bound on the sum of `block_mask` on one device may be relied on, other than what follows from the above.
Results may differ from a plain program's by a relative error of at most 0.0001.
Values sent between devices are 32-bit elements; how exact they have to be, the bound alone decides.
A program may use at most 64 MiB of HBM per device.

v0:
```python
import jax
import jax.numpy as jnp
from jax import lax
from jax.sharding import PartitionSpec as P


def mask_rows(factor_rows, block_mask, row_start, block_size):
    row_total = factor_rows.shape[1]
    block_count = block_mask.shape[3]
    row_blocks = (row_start + jnp.arange(row_total, dtype=jnp.int32)) // block_size
    row_select = (row_blocks[:, None] == jnp.arange(block_count, dtype=jnp.int32)[None, :]).astype(
        jnp.float32
    )
    row_masks = jnp.einsum("rk,pkc->prc", row_select, block_mask[0].astype(jnp.float32))
    return factor_rows * jnp.repeat(row_masks, block_size, axis=2)


def group_reduce(partial_value):
    summed = lax.psum_scatter(partial_value, "depth", scatter_dimension=0, tiled=True)
    return summed[0]


def group_collect(spread):
    every_rows = lax.all_gather(spread[None], "depth", axis=0, tiled=True)
    return every_rows


def invert_level(inverse_block, own_rows):
    inverse_term = jnp.dot(
        inverse_block, own_rows, precision=lax.Precision.HIGHEST, preferred_element_type=jnp.float32
    )
    return lax.psum(inverse_term, "rows")


def per_device(sources, factor, block_mask, inverse_diagonal):
    depth_count = lax.axis_size("depth")
    tree_height = depth_count.bit_length() - 1
    level_count = tree_height + 1
    shot_index = lax.axis_index("shots")
    rows_index = lax.axis_index("rows")
    thin_rows = factor.shape[2]
    full_width = factor.shape[3]
    block_count = block_mask.shape[3]
    block_size = full_width // block_count
    highest = lax.Precision.HIGHEST
    row_start = (rows_index * lax.axis_size("shots") + shot_index) * thin_rows
    masked = mask_rows(factor[0], block_mask, row_start, block_size)
    solved = []
    wide_solved = []
    for tier_index in range(level_count):
        own_rows = sources[0, tier_index]
        if tier_index > 0:
            group_size = 2**tier_index
            factor_tiles = masked.reshape(tier_index, group_size, thin_rows, full_width)
            lower_solved = jnp.stack(wide_solved[:tier_index])
            partial_value = jnp.einsum(
                "lgrs,lsn->grn",
                factor_tiles,
                lower_solved,
                precision=highest,
                preferred_element_type=jnp.float32,
            )
            reduced = group_reduce(partial_value)
            reduced = lax.all_to_all(reduced, "shots", split_axis=1, concat_axis=0, tiled=True)
            own_rows = own_rows - reduced
        full_rows = invert_level(inverse_diagonal[0, tier_index], own_rows)
        solved.append(full_rows)
        if tier_index < tree_height:
            wide_solved.append(lax.all_gather(full_rows, "shots", axis=1, tiled=True))
    answers = [None] * level_count
    collected = {}
    for tier_index in reversed(range(level_count)):
        target = solved[tier_index]
        if tier_index < tree_height:
            factor_tiles = masked
            transposed = jnp.einsum(
                "grs,grn->sn",
                factor_tiles,
                collected[1],
                precision=highest,
                preferred_element_type=jnp.float32,
            )
            shot_piece = lax.psum_scatter(transposed, "shots", scatter_dimension=1, tiled=True)
            own_columns = lax.psum(shot_piece, "rows")
            target = target - own_columns
        answer = lax.dot_general(
            inverse_diagonal[0, tier_index],
            target,
            (((0,), (0,)), ((), ())),
            precision=highest,
            preferred_element_type=jnp.float32,
        )
        answers[tier_index] = answer
        if tier_index > 0:
            spread = lax.all_to_all(answer, "shots", split_axis=0, concat_axis=1, tiled=True)
            collected[tier_index] = group_collect(spread)
    return jnp.stack(answers)[None]


def solution(mesh):
    placed = (
        P("depth", None, "rows", "shots"),
        P("depth", None, ("rows", "shots"), None),
        P("depth", None, None, None),
        P("depth", None, None, "rows"),
    )
    return jax.shard_map(
        per_device,
        mesh=mesh,
        in_specs=placed,
        out_specs=P("depth", None, "rows", "shots"),
        check_vma=False,
    )
```

profile of v0, /device:TPU:0, one launch (start us, length us, event | category | flops | bytes accessed | tf_op | source)
XLA Modules:
  0.0 941.2 jit_solution(3403991604582665466)
XLA Ops:
  6.5 4.2 fusion.8
  10.8 0.0 all-gather.2.cloned.1.call-start
  10.8 39.2 %all-reduce.4.cloned.1.call-done = f32[1024,128]{1,0:T(8,128)} async-done(((f32[1024,128]{1,0:T(8,128)}), f32[1024,128]{1,0:T(8,128)}) %all-reduce.4.cloned.1.call-update) | async-done | bytes 524304 | tf_op jit(solution)/shard_map/psum | solution.py:32
  50.1 0.0 reduce-scatter.3.cloned.1.call-start
  50.1 0.7 convert_bitcast_fusion
  50.8 0.1 copy.15
  50.9 0.1 convolution_bitcast_fusion.1
  51.1 0.1 copy.16
  51.1 0.1 broadcast_in_dim.11
  51.3 359.2 %all-gather.2.cloned.1.call-done = f32[1024,4096]{1,0:T(8,128)} async-done(((f32[1024,128]{1,0:T(8,128)}), f32[1024,4096]{1,0:T(8,128)}) %all-gather.2.cloned.1.call-update) | async-done | bytes 16777232 | tf_op jit(solution)/shard_map/all_gather | solution.py:69
  410.5 13.9 %fusion = f32[2,16,4096]{2,1,0:T(8,128)} fusion(f32[1024,4096]{1,0:T(8,128)} %all-gather.2.cloned.1.call-done, f32[1,2,16,1024]{3,2,1,0:T(8,128)S(1)} %copy-done.1, f32[1,2,16,1024]{3,2,1,0:T(8,128)S(1)} %reshape.43), kind=kOutput, calls=%fused_computation | convolution fusion | flops 1610645504 | bytes 17563648 | tf_op jit(solution)/shard_map/lgrs,lsn->grn/dot_general | solution.py:56
  424.4 0.0 all-reduce.6.cloned.1.call-start
  424.5 11.6 %reduce-scatter.3.cloned.1.call-done = f32[1,16,4096]{2,1,0:T(8,128)} async-done(((f32[2,16,4096]{2,1,0:T(8,128)}), f32[1,16,4096]{2,1,0:T(8,128)}) %reduce-scatter.3.cloned.1.call-update) | async-done | bytes 262160 | tf_op jit(solution)/shard_map/reduce_scatter | solution.py:19
  436.0 1.0 copy.21
  437.0 0.2 copy.17
  437.2 18.1 %all_to_all.35 = f32[16,32,128]{2,0,1:T(8,128)S(1)} all-to-all(f32[16,32,128]{2,0,1:T(8,128)S(1)} %copy.17), channel_id=1, replica_groups=mesh['depth'=2,'rows'=2,'shots'=32] {'shots'}, dimensions={1} | all-to-all | bytes 524288 | tf_op jit(solution)/shard_map/all_to_all | solution.py:64
  455.3 4.7 fusion.14
  460.0 34.2 %all-reduce.6.cloned.1.call-done = f32[1024,128]{0,1:T(8,128)} async-done(((f32[1024,128]{0,1:T(8,128)}), f32[1024,128]{0,1:T(8,128)}) %all-reduce.6.cloned.1.call-update) | async-done | bytes 524304 | tf_op jit(solution)/shard_map/psum | solution.py:32
  494.2 3.1 fusion.2
  497.3 0.8 copy.18
  498.1 7.3 all-to-all-start.1
  505.4 0.0 reduce-scatter.5.cloned.1.call-start
  505.5 9.3 all-to-all-done.1
  514.8 0.1 copy.19
  514.9 0.1 broadcast_in_dim.12
  514.9 2.4 all_gather.7
  517.3 16.0 %convolution_bitcast_fusion = f32[1024,4096]{1,0:T(8,128)} fusion(f32[2,16,4096]{2,1,0:T(8,128)S(1)} %all_gather.7, f32[2,16,1024]{2,1,0:T(8,128)S(1)} %reshape.42, f32[1,2,16,1024]{3,2,1,0:T(8,128)S(1)} %copy-done.1), kind=kOutput, calls=%fused_computation.2 | convolution fusion | flops 1610645504 | bytes 17563648 | tf_op jit(solution)/shard_map/grs,grn->sn/dot_general | solution.py:76
  533.3 0.0 all-reduce.8.cloned.1.call-start
  533.3 360.1 %reduce-scatter.5.cloned.1.call-done = f32[1024,128]{1,0:T(8,128)} async-done(((f32[1024,4096]{1,0:T(8,128)}), f32[1024,128]{1,0:T(8,128)}) %reduce-scatter.5.cloned.1.call-update) | async-done | bytes 524304 | tf_op jit(solution)/shard_map/reduce_scatter | solution.py:83
  893.5 36.7 %all-reduce.8.cloned.1.call-done = f32[1024,128]{1,0:T(8,128)} async-done(((f32[1024,128]{1,0:T(8,128)}), f32[1024,128]{1,0:T(8,128)}) %all-reduce.8.cloned.1.call-update) | async-done | bytes 524304 | tf_op jit(solution)/shard_map/psum | solution.py:84
  930.2 3.2 fusion.17
  933.4 1.0 copy.20
  (17 shorter events, 0.2 us)
Async XLA Ops:
  6.5 404.0 %copy-start.1 = (f32[1,2,16,1024]{3,2,1,0:T(8,128)S(1)}, f32[1,2,16,1024]{3,2,1,0:T(8,128)}, u32[]{:S(2)}) copy-start(f32[1,2,16,1024]{3,2,1,0:T(8,128)} %param.5) | copy-start | bytes 393220
  6.5 43.5 %all-reduce.4.cloned.1.call-start = ((), (), s32[]{:S(2)}) async-start(), calls=%async_computation.4 | async-start | bytes 1048576 | tf_op jit(solution)/shard_map/psum | solution.py:32
  10.8 399.7 %all-gather.2.cloned.1.call-start = ((), (), s32[]{:S(2)}) async-start(), calls=%async_computation.5 | async-start | bytes 17301504 | tf_op jit(solution)/shard_map/all_gather | solution.py:69
  50.1 385.9 %reduce-scatter.3.cloned.1.call-start = ((), (), s32[]{:S(2)}) async-start(), calls=%async_computation.6 | async-start | bytes 786432 | tf_op jit(solution)/shard_map/reduce_scatter | solution.py:19
  51.3 404.0 %copy-start.2 = (f32[1,2,512,128]{3,2,1,0:T(8,128)S(1)}, f32[1,2,512,128]{3,2,1,0:T(8,128)}, u32[]{:S(2)}) copy-start(f32[1,2,512,128]{3,2,1,0:T(8,128)} %param.4) | copy-start | bytes 1572868
  424.4 69.8 %all-reduce.6.cloned.1.call-start = ((), (), s32[]{:S(2)}) async-start(), calls=%async_computation.7 | async-start | bytes 1048576 | tf_op jit(solution)/shard_map/psum | solution.py:32
  498.1 16.7 %all-to-all-start.1 = ((f32[32,16,128]{2,1,0:T(8,128)}), f32[32,16,128]{2,1,0:T(8,128)S(1)}, u32[]{:S(2)}, u32[]{:S(2)}) async-start(f32[32,16,128]{2,1,0:T(8,128)} %bitcast.16), calls=%async_computation.2 | async-start | bytes 524288 | tf_op jit(solution)/shard_map/all_to_all | solution.py:95
  505.4 388.1 %reduce-scatter.5.cloned.1.call-start = ((), (), s32[]{:S(2)}) async-start(), calls=%async_computation.8 | async-start | bytes 17301504 | tf_op jit(solution)/shard_map/reduce_scatter | solution.py:83
  533.3 396.9 %copy-start = (f32[1024,128]{1,0:T(8,128)S(1)}, f32[1024,128]{1,0:T(8,128)}, u32[]{:S(2)}) copy-start(f32[1024,128]{1,0:T(8,128)} %all-reduce.4.cloned.1.call-done) | copy-start | bytes 1572868
  533.3 396.9 %all-reduce.8.cloned.1.call-start = ((), (), s32[]{:S(2)}) async-start(), calls=%async_computation.9 | async-start | bytes 1048576 | tf_op jit(solution)/shard_map/psum | solution.py:84
Sparse Core Ops, SparseCore 0:
  10.9 39.1 all-reduce.3
  51.7 358.7 all-gather.1
  424.5 11.4 reduce-scatter.2
  460.1 34.0 all-reduce.5
  533.4 359.9 reduce-scatter.4
  895.9 34.2 all-reduce.7
where the time goes:
time: 942 us; the launch traced here: 941 us
  waiting for transfers between devices  850 us (90%)
  matrix products  45.1 us (5%)
  blocking collectives  20.4 us (2%)
  between operations  13.6 us (1%)
    reduce_scatter x1, waiting for transfers between devices, per_device(): lax.psum_scatter(transposed, 'shots', scatter_dimension=1, tiled=True)  360 us
    all_gather x1, waiting for transfers between devices, per_device(): wide_solved.append(lax.all_gather(full_rows, 'shots', axis=1, tiled=True))  359 us
    psum x2, waiting for transfers between devices, invert_level(): return lax.psum(inverse_term, 'rows')  73.4 us
    psum x1, waiting for transfers between devices, per_device(): own_columns = lax.psum(shot_piece, 'rows')  36.7 us
  transfers between devices with their start and end apart: 7, of which 7 were waited for; matrix products, arithmetic and copies ran while one was open for 0% of the time, Pallas kernels for 0%

commit v1 on v0

v1 whole, which is shorter than its diff:
```python
import jax
import jax.numpy as jnp
from jax import lax
from jax.sharding import PartitionSpec as P


def mask_rows(factor_rows, block_mask, row_start, block_size):
    row_total = factor_rows.shape[1]
    block_count = block_mask.shape[3]
    row_blocks = (row_start + jnp.arange(row_total, dtype=jnp.int32)) // block_size
    row_select = (row_blocks[:, None] == jnp.arange(block_count, dtype=jnp.int32)[None, :]).astype(
        jnp.float32
    )
    row_masks = jnp.einsum("rk,pkc->prc", row_select, block_mask[0].astype(jnp.float32))
    return factor_rows * jnp.repeat(row_masks, block_size, axis=2)


def product(spec, left, right):
    return jnp.einsum(
        spec, left, right, precision=lax.Precision.HIGH, preferred_element_type=jnp.float32
    )


def per_device(sources, factor, block_mask, inverse_diagonal):
    shot_index = lax.axis_index("shots")
    rows_index = lax.axis_index("rows")
    thin_rows = factor.shape[2]
    full_width = factor.shape[3]
    block_size = full_width // block_mask.shape[3]
    row_start = (rows_index * lax.axis_size("shots") + shot_index) * thin_rows
    masked = mask_rows(factor[0], block_mask, row_start, block_size)
    tiles = lax.all_gather(masked, "shots", axis=1, tiled=True)
    low = lax.psum(product("rs,sn->rn", inverse_diagonal[0, 0], sources[0, 0]), "rows")
    update = product("trs,sn->trn", tiles, low)
    own = sources[0, 1] - lax.psum_scatter(update, "depth", scatter_dimension=0, tiled=True)[0]
    high = lax.psum(product("rs,sn->rn", inverse_diagonal[0, 1], own), "rows")
    top = product("sr,sn->rn", inverse_diagonal[0, 1], high)
    tops = lax.all_gather(top[None], "depth", axis=0, tiled=True)
    target = low - lax.psum(product("trs,trn->sn", tiles, tops), "rows")
    bottom = product("sr,sn->rn", inverse_diagonal[0, 0], target)
    return jnp.stack([bottom, top])[None]


def solution(mesh):
    placed = (
        P("depth", None, "rows", "shots"),
        P("depth", None, ("rows", "shots"), None),
        P("depth", None, None, None),
        P("depth", None, None, "rows"),
    )
    return jax.shard_map(
        per_device,
        mesh=mesh,
        in_specs=placed,
        out_specs=P("depth", None, "rows", "shots"),
        check_vma=False,
    )
```

time: 942 us -> 303 us (0.32)
  waiting for transfers between devices: 850 us -> 258 us
  matrix products: 45.1 us -> 23.5 us
  blocking collectives: 20.4 us -> 2.31 us
    reduce_scatter x2 -> x1, waiting for transfers between devices: 372 us -> 8.44 us  [per_device(): lax.psum_scatter(update, 'depth', scatter_dimension=0, tiled=True)[0]]
    all_gather x1, waiting for transfers between devices: 359 us -> 137 us  [per_device(): tiles = lax.all_gather(masked, 'shots', axis=1, tiled=True)]
    dot_general x6, matrix products: 45 us -> 23.4 us  [product(): jnp.einsum(spec, left, right, precision=lax.Precision.HIGH, preferred_ele...]
    all_to_all x1 -> x0, blocking collectives: 18.1 us -> none  [per_device(): lax.all_to_all(reduced, 'shots', split_axis=1, concat_axis=0, tiled=True)]
  transfers between devices with their start and end apart: 7 -> 5, of which waited for: 7 -> 5; matrix products, arithmetic and copies ran while one was open for 0% -> 1% of each run, Pallas kernels for 0% -> 0%
where the time goes in v1:
time: 303 us; the launch traced here: 302 us
  waiting for transfers between devices  258 us (85%)
  matrix products  23.5 us (8%)
  between operations  14.6 us (5%)
    all_gather x1, waiting for transfers between devices, per_device(): tiles = lax.all_gather(masked, 'shots', axis=1, tiled=True)  137 us
    psum x1, waiting for transfers between devices, per_device(): high = lax.psum(product('rs,sn->rn', inverse_diagonal[0, 1], own), 'rows')  38.3 us
    psum x1, waiting for transfers between devices, per_device(): lax.psum(product('rs,sn->rn', inverse_diagonal[0, 0], sources[0, 0]), 'ro...  37.9 us
    psum x1, waiting for transfers between devices, per_device(): target = low - lax.psum(product('trs,trn->sn', tiles, tops), 'rows')  36.3 us
    dot_general x6, matrix products, product(): jnp.einsum(spec, left, right, precision=lax.Precision.HIGH, preferred_ele...  23.4 us
    reduce_scatter x1, waiting for transfers between devices, per_device(): lax.psum_scatter(update, 'depth', scatter_dimension=0, tiled=True)[0]  8.44 us
  transfers between devices with their start and end apart: 5, of which 5 were waited for; matrix products, arithmetic and copies ran while one was open for 1% of the time, Pallas kernels for 0%

profile of v1, /device:TPU:0, one launch (start us, length us, event | category | flops | bytes accessed | tf_op | source)
XLA Modules:
  0.0 302.3 jit_solution(8039582276913375339)
XLA Ops:
  7.4 0.0 all-reduce.4.cloned.1.call-start
  7.4 3.4 %fusion.6 = f32[1024,128]{1,0:T(8,128)} fusion(f32[1,2,1024,512]{3,2,1,0:T(8,128)} %param.7, f32[1,2,512,128]{3,2,1,0:T(8,128)} %param.4), kind=kOutput, calls=%fused_computation.6 | convolution fusion | flops 402653184 | bytes 2883584 | tf_op jit(solution)/shard_map/rs,sn->rn/dot_general | solution.py:19
  10.7 0.0 all-reduce.4.cloned.1.call-update
  10.8 0.0 all-gather.3.cloned.1.call-start
  10.8 0.7 convert_bitcast_fusion
  11.6 0.1 copy.5
  11.7 0.1 convolution_bitcast_fusion.1
  11.8 0.1 copy.6
  11.9 0.1 broadcast_in_dim.11
  12.0 1.6 bitcast_multiply_fusion
  13.6 0.0 all-gather.3.cloned.1.call-update
  13.6 0.0 reduce-scatter.2.cloned.1.call-start
  13.6 37.9 %all-reduce.4.cloned.1.call-done = f32[1024,128]{1,0:T(8,128)} async-done(((f32[1024,128]{1,0:T(8,128)}), f32[1024,128]{1,0:T(8,128)}) %all-reduce.4.cloned.1.call-update) | async-done | bytes 524304 | tf_op jit(solution)/shard_map/psum | solution.py:33
  51.6 136.9 %all-gather.3.cloned.1.call-done = f32[2,512,1024]{2,1,0:T(8,128)} async-done(((f32[2,16,1024]{2,1,0:T(8,128)}), f32[2,512,1024]{2,1,0:T(8,128)}) %all-gather.3.cloned.1.call-update) | async-done | bytes 4194320 | tf_op jit(solution)/shard_map/all_gather | solution.py:32
  188.5 4.9 %fusion.18 = f32[2,512,128]{2,1,0:T(8,128)} fusion(f32[2,512,1024]{2,1,0:T(8,128)} %all-gather.3.cloned.1.call-done, f32[1024,128]{1,0:T(8,128)} %all-reduce.4.cloned.1.call-done), kind=kOutput, calls=%fused_computation.17 | convolution fusion | flops 805306368 | bytes 5242880 | tf_op jit(solution)/shard_map/trs,sn->trn/dot_general | solution.py:19
  193.4 0.0 reduce-scatter.2.cloned.1.call-update
  193.4 0.0 all-reduce.6.cloned.1.call-start
  193.4 8.4 %reduce-scatter.2.cloned.1.call-done = f32[1,512,128]{2,1,0:T(8,128)} async-done(((f32[2,512,128]{2,1,0:T(8,128)}), f32[1,512,128]{2,1,0:T(8,128)}) %reduce-scatter.2.cloned.1.call-update) | async-done | bytes 262160 | tf_op jit(solution)/shard_map/reduce_scatter | solution.py:35
  201.9 0.0 copy-done.1
  201.9 3.7 %fusion.12 = f32[1024,128]{0,1:T(8,128)} fusion(f32[1,2,1024,512]{3,2,1,0:T(8,128)} %param.7, f32[1,512,128]{2,1,0:T(8,128)} %reduce-scatter.2.cloned.1.call-done, f32[1,2,512,128]{3,2,1,0:T(8,128)S(1)} %copy-done.1), kind=kOutput, calls=%fused_computation.12 | convolution fusion | flops 402718720 | bytes 3145728 | tf_op jit(solution)/shard_map/rs,sn->rn/dot_general | solution.py:19
  205.6 0.0 all-reduce.6.cloned.1.call-update
  205.6 0.0 all-reduce.8.cloned.1.call-start
  205.7 38.3 %all-reduce.6.cloned.1.call-done = f32[1024,128]{0,1:T(8,128)} async-done(((f32[1024,128]{0,1:T(8,128)}), f32[1024,128]{0,1:T(8,128)}) %all-reduce.6.cloned.1.call-update) | async-done | bytes 524304 | tf_op jit(solution)/shard_map/psum | solution.py:36
  243.9 2.5 fusion
  246.4 0.0 copy-start
  246.4 2.3 all-gather
  248.7 0.2 copy.9
  248.9 6.4 %convolution_bitcast_fusion = f32[1024,128]{1,0:T(8,128)} fusion(f32[2,512,1024]{2,1,0:T(8,128)} %all-gather.3.cloned.1.call-done, f32[2,512,128]{2,1,0:T(8,128)S(1)} %bitcast.63), kind=kOutput, calls=%fused_computation.13 | convolution fusion | flops 805306368 | bytes 5242880 | tf_op jit(solution)/shard_map/trs,trn->sn/dot_general | solution.py:19
  255.3 0.0 all-reduce.8.cloned.1.call-update
  255.4 36.3 %all-reduce.8.cloned.1.call-done = f32[1024,128]{1,0:T(8,128)} async-done(((f32[1024,128]{1,0:T(8,128)}), f32[1024,128]{1,0:T(8,128)}) %all-reduce.8.cloned.1.call-update) | async-done | bytes 524304 | tf_op jit(solution)/shard_map/psum | solution.py:39
  291.6 2.5 fusion.15
  294.2 1.0 copy.7
  (5 shorter events, 0.1 us)
Async XLA Ops:
  7.4 44.2 %all-reduce.4.cloned.1.call-start = ((), (), s32[]{:S(2)}) async-start(), calls=%async_computation.1 | async-start | bytes 1048576 | tf_op jit(solution)/shard_map/psum | solution.py:33
  10.7 191.1 %copy-start.1 = (f32[1,2,512,128]{3,2,1,0:T(8,128)S(1)}, f32[1,2,512,128]{3,2,1,0:T(8,128)}, u32[]{:S(2)}) copy-start(f32[1,2,512,128]{3,2,1,0:T(8,128)} %param.4) | copy-start | bytes 1572868
  10.8 177.7 %all-gather.3.cloned.1.call-start = ((), (), s32[]{:S(2)}) async-start(), calls=%async_computation.2 | async-start | bytes 4325376 | tf_op jit(solution)/shard_map/all_gather | solution.py:32
  13.6 188.3 %reduce-scatter.2.cloned.1.call-start = ((), (), s32[]{:S(2)}) async-start(), calls=%async_computation.3 | async-start | bytes 786432 | tf_op jit(solution)/shard_map/reduce_scatter | solution.py:35
  193.4 50.5 %all-reduce.6.cloned.1.call-start = ((), (), s32[]{:S(2)}) async-start(), calls=%async_computation.4 | async-start | bytes 1048576 | tf_op jit(solution)/shard_map/psum | solution.py:36
  205.6 86.0 %all-reduce.8.cloned.1.call-start = ((), (), s32[]{:S(2)}) async-start(), calls=%async_computation.5 | async-start | bytes 1048576 | tf_op jit(solution)/shard_map/psum | solution.py:39
  246.4 45.2 %copy-start = (f32[1024,128]{1,0:T(8,128)S(1)}, f32[1024,128]{1,0:T(8,128)}, u32[]{:S(2)}) copy-start(f32[1024,128]{1,0:T(8,128)} %all-reduce.4.cloned.1.call-done) | copy-start | bytes 1572868
Sparse Core Ops, SparseCore 0:
  10.9 40.6 all-reduce.3
  193.5 8.3 reduce-scatter.1
  205.7 38.1 all-reduce.5
  255.5 36.0 all-reduce.7
Sparse Core Ops, SparseCore 1:
  13.7 174.7 all-gather.2

commit v2 on v1

v2 whole, which is shorter than its diff:
```python
import jax
import jax.numpy as jnp
from jax import lax
from jax.experimental import pallas as pl
from jax.experimental.pallas import tpu as pltpu
from jax.sharding import PartitionSpec as P

MESH = pl.DeviceIdType.MESH
F32 = jnp.float32
BF16 = jnp.bfloat16
BLOCK = 128
HALF = 512
FULL = 1024
SHOTS = 128


def split(x):
    high = x.astype(BF16)
    return high, (x - high.astype(F32)).astype(BF16)


def dot(a, b):
    return jnp.dot(a, b, preferred_element_type=F32)


def wide_product(a_high, a_low, b_pair):
    both = dot(a_high, b_pair)
    return both[:, :SHOTS] + both[:, SHOTS:] + dot(a_low, b_pair[:, :SHOTS])


def tall_product(a_pair, b_high, b_low):
    both = dot(a_pair, b_high)
    return both[:SHOTS] + both[SHOTS:] + dot(a_pair[:SHOTS], b_low)


class Copies:
    def __init__(self, send_sems, recv_sems):
        self.send_sems, self.recv_sems, self.count, self.sent = send_sems, recv_sems, 0, []

    def slot(self):
        self.count += 1
        return self.count - 1

    def make(self, slot, src, dst, device):
        return pltpu.make_async_remote_copy(
            src_ref=src,
            dst_ref=dst,
            send_sem=self.send_sems.at[slot],
            recv_sem=self.recv_sems.at[slot],
            device_id=device,
            device_id_type=MESH,
        )

    def send(self, slot, src, dst, device):
        copy = self.make(slot, src, dst, device)
        copy.start()
        self.sent.append(copy)

    def arrived(self, slot, dst, device):
        self.make(slot, dst, dst, device).wait_recv()

    def finish(self):
        for copy in self.sent:
            copy.wait_send()


COPIES = 104


def kernel(
    src_hbm,
    fac_hbm,
    mask_ref,
    inv_hbm,
    out_ref,
    src,
    fac,
    inv,
    tiles,
    tiles_high,
    tiles_low,
    inv_high,
    inv_low,
    low,
    low_in,
    low_pair,
    low_t,
    update,
    update_in,
    high_out,
    high_in,
    top_t,
    part_t,
    part_in,
    load_sems,
    send_sems,
    recv_sems,
):
    core = lax.axis_index("depth")
    row = lax.axis_index("rows")
    shot = lax.axis_index("shots")
    zy, xl = shot // 2, shot % 2
    z, y = zy // 4, zy % 4

    def at(dz, dy):
        return ((z + dz) % 4) * 4 + (y + dy) % 4

    def place(axis, step):
        return at(step, 0) if axis == 0 else at(0, step)

    def neighbour(axis, step):
        return (core, row, place(axis, step) * 2 + xl)

    beside = (core, row, zy * 2 + 1 - xl)
    across = (core, 1 - row, shot)
    twin = (1 - core, row, shot)

    loads = [
        pltpu.make_async_copy(fac_hbm.at[0], fac, load_sems.at[0]),
        pltpu.make_async_copy(src_hbm.at[0], src, load_sems.at[1]),
        pltpu.make_async_copy(inv_hbm.at[0, 0], inv.at[0], load_sems.at[2]),
        pltpu.make_async_copy(inv_hbm.at[0, 1], inv.at[1], load_sems.at[3]),
    ]
    for load in loads:
        load.start()

    barrier = pltpu.get_barrier_semaphore()
    partners = [neighbour(a, s) for a in (0, 1) for s in (1, -1)] + [beside, across, twin]
    for partner in partners:
        pl.semaphore_signal(barrier, inc=1, device_id=partner, device_id_type=MESH)

    loads[0].wait()
    row_block = row * 4 + zy // 4
    for t in range(2):
        for k in range(8):
            scale = mask_ref[0, t, row_block, k].astype(F32)
            piece = fac[t, :, k * BLOCK : (k + 1) * BLOCK] * scale
            tiles[t, k // 4, zy, xl, :, (k % 4) * BLOCK : (k % 4 + 1) * BLOCK] = piece

    pl.semaphore_wait(barrier, len(partners))

    copies = Copies(send_sems, recv_sems)
    parts = [(t, h) for t in range(2) for h in range(2)]
    first = {h: 1 - h for h in range(2)}
    slot_x = {p: copies.slot() for p in parts}
    slot_own = {(p, s): copies.slot() for p in parts for s in (1, -1)}
    slot_side = {(p, s): copies.slot() for p in parts for s in (1, -1)}
    slot_far = {(p, s): copies.slot() for p in parts for s in (1, -1)}
    units = (0, -1, 1, 2)
    slot_two = {(p, u, s): copies.slot() for p in parts for u in units for s in (1, -1)}
    slot_two_far = {(p, u, s): copies.slot() for p in parts for u in units for s in (1, -1)}
    slot_low = [copies.slot() for _ in range(2)]
    slot_update = copies.slot()
    slot_high = copies.slot()
    slot_top = copies.slot()
    slot_part = [copies.slot() for _ in range(4)]
    assert copies.count <= COPIES

    def unit_place(h, u, s):
        return at(s, u) if first[h] == 1 else at(u, s)

    def swap_beside(p):
        t, h = p
        piece = tiles.at[t, h, zy, xl]
        copies.send(slot_x[p], piece, piece, beside)

    def send_own(p):
        t, h = p
        piece = tiles.at[t, h, zy, xl]
        for s in (1, -1):
            copies.send(slot_own[p, s], piece, piece, neighbour(first[h], s))

    def wait_beside(p):
        t, h = p
        copies.arrived(slot_x[p], tiles.at[t, h, zy, 1 - xl], beside)

    def send_side(p):
        t, h = p
        piece = tiles.at[t, h, zy, 1 - xl]
        for s in (1, -1):
            copies.send(slot_side[p, s], piece, piece, neighbour(first[h], s))

    def send_unit(p, u):
        t, h = p
        piece = tiles.at[t, h, unit_place(h, u, 0)]
        for s in (1, -1):
            copies.send(slot_two[p, u, s], piece, piece, neighbour(1 - first[h], s))

    def relay_one(p, s):
        t, h = p
        where = unit_place(h, -s, 0)
        copies.arrived(slot_own[p, s], tiles.at[t, h, where, xl], neighbour(first[h], -s))
        copies.arrived(slot_side[p, s], tiles.at[t, h, where, 1 - xl], neighbour(first[h], -s))
        piece = tiles.at[t, h, where, 0 if s == 1 else 1]
        copies.send(slot_far[p, s], piece, piece, neighbour(first[h], s))

    def wait_far(p):
        t, h = p
        for s in (1, -1):
            piece = tiles.at[t, h, unit_place(h, 2, 0), 0 if s == 1 else 1]
            copies.arrived(slot_far[p, s], piece, neighbour(first[h], -s))

    def relay_two(p, u):
        t, h = p
        for s in (1, -1):
            where = unit_place(h, u, -s)
            copies.arrived(slot_two[p, u, s], tiles.at[t, h, where], neighbour(1 - first[h], -s))
            piece = tiles.at[t, h, where, 0 if s == 1 else 1]
            copies.send(slot_two_far[p, u, s], piece, piece, neighbour(1 - first[h], s))

    def wait_two_far(p, u):
        t, h = p
        for s in (1, -1):
            piece = tiles.at[t, h, unit_place(h, u, 2), 0 if s == 1 else 1]
            copies.arrived(slot_two_far[p, u, s], piece, neighbour(1 - first[h], -s))

    def pair(t):
        return [(t, 0), (t, 1)]

    for p in parts:
        swap_beside(p)
    for p in pair(0):
        send_own(p)

    def invert_split(m):
        loads[2 + m].wait()

        @pl.loop(0, 4)
        def _(i):
            rows = pl.ds(pl.multiple_of(i * 256, 256), 256)
            inv_high[m, rows], inv_low[m, rows] = split(inv[m, rows])

    loads[1].wait()
    invert_split(0)
    for p in pair(0):
        wait_beside(p)
        send_side(p)
        send_unit(p, 0)
    source_pair = jnp.concatenate(split(src[0]), axis=1)

    @pl.loop(0, 4)
    def _(i):
        rows = pl.ds(pl.multiple_of(i * 256, 256), 256)
        low[rows] = wide_product(inv_high[0, rows], inv_low[0, rows], source_pair)

    bottom, upper = pl.ds(HALF, HALF), pl.ds(0, HALF)
    copies.send(slot_low[1], low.at[bottom], low_in.at[bottom], across)

    @pl.when(row == 0)
    def _():
        copies.make(slot_low[0], low.at[upper], low_in.at[upper], across).start()

    for p in pair(0):
        for s in (1, -1):
            relay_one(p, s)
        send_unit(p, -1)
        send_unit(p, 1)
    for p in pair(1):
        send_own(p)
        wait_beside(p)
        send_side(p)
        send_unit(p, 0)
    for p in pair(0):
        wait_far(p)
        send_unit(p, 2)
    invert_split(1)
    for p in pair(0):
        relay_two(p, 0)
    for p in pair(1):
        for s in (1, -1):
            relay_one(p, s)
        send_unit(p, -1)
        send_unit(p, 1)
    for p in pair(0):
        relay_two(p, -1)
        relay_two(p, 1)
    for p in pair(1):
        wait_far(p)
        send_unit(p, 2)
    for p in pair(0):
        relay_two(p, 2)
    for p in pair(1):
        relay_two(p, 0)

    copies.arrived(slot_low[1], low_in.at[bottom], across)

    @pl.when(row == 1)
    def _():
        copies.arrived(slot_low[0], low_in.at[upper], across)

    @pl.when(row == 0)
    def _():
        low_in[upper] = low[upper]

    low_in[bottom] = low[bottom] + low_in[bottom]
    low_pair[...] = jnp.concatenate(split(low_in[...]), axis=1)
    low_t[...] = low_in[...].T

    for p in pair(1):
        relay_two(p, -1)
        relay_two(p, 1)

    def forward(t):
        @pl.loop(0, 4)
        def _(i):
            rows = pl.ds(pl.multiple_of(i * 128, 128), 128)
            total = jnp.zeros((128, SHOTS), F32)
            for h in range(2):
                block = tiles[t, h, pl.ds(i * 4, 4)].reshape(128, HALF)
                high, rest = split(block)
                cols = pl.ds(h * HALF, HALF)
                tiles_high[t, rows, cols] = high
                tiles_low[t, rows, cols] = rest
                total += wide_product(high, rest, low_pair[cols])
            update[t, rows] = total

    def level_one(t):
        @pl.when(core != t)
        def _():
            copy = copies.make(slot_update, update.at[t], update_in, twin)
            copy.start()
            copy.wait_send()
            copies.arrived(slot_top, top_t, twin)

        @pl.when(core == t)
        def _():
            copies.arrived(slot_update, update_in, twin)
            own_pair = jnp.concatenate(split(src[1] - update[t] - update_in[...]), axis=1)

            @pl.loop(0, 4)
            def _(i):
                rows = pl.ds(pl.multiple_of(i * 256, 256), 256)
                high_out[rows] = wide_product(inv_high[1, rows], inv_low[1, rows], own_pair)

            copy = copies.make(slot_high, high_out.at[bottom], high_in, across)
            copy.start()
            upper_pair = jnp.concatenate(split(high_out[upper].T), axis=0)
            total = tall_product(upper_pair, inv_high[1, upper], inv_low[1, upper])
            copy.wait()
            lower_pair = jnp.concatenate(split((high_out[bottom] + high_in[...]).T), axis=0)
            total += tall_product(lower_pair, inv_high[1, bottom], inv_low[1, bottom])
            top_t[...] = total
            copy = copies.make(slot_top, top_t, top_t, twin)
            copy.start()
            out_ref[0, 1] = total.T
            copy.wait_send()

    def backward(t):
        top_pair = jnp.concatenate(split(top_t[...]), axis=0)
        for k in range(4):
            cols = pl.ds(k * 256, 256)
            share = tall_product(top_pair, tiles_high[t, :, cols], tiles_low[t, :, cols])
            part_t[k] = share if t == 0 else part_t[k] + share

    for p in pair(0):
        for u in units:
            wait_two_far(p, u)
    for p in pair(1):
        relay_two(p, 2)
    for p in pair(1):
        for u in units:
            wait_two_far(p, u)
    for t in range(2):
        forward(t)
    for t in range(2):
        level_one(t)
        backward(t)

    for k in (2, 3):
        copies.send(slot_part[k], part_t.at[k], part_in.at[k], across)

    @pl.when(row == 1)
    def _():
        for k in (0, 1):
            copies.make(slot_part[k], part_t.at[k], part_in.at[k], across).start()

    def final(k):
        cols = pl.ds(k * 256, 256)
        copies.arrived(slot_part[k], part_in.at[k], across)
        target = low_t[:, cols] - part_t[k] - part_in[k]
        pair_ = jnp.concatenate(split(target), axis=0)
        return tall_product(pair_, inv_high[0, cols], inv_low[0, cols])

    answer = final(2) + final(3)
    low_in[pl.ds(0, HALF)] = answer.T

    @pl.when(row == 0)
    def _():
        more = final(0) + final(1)
        low_in[pl.ds(0, HALF)] = low_in[pl.ds(0, HALF)] + more.T

    out_ref[0, 0] = low_in[pl.ds(0, HALF)]

    copies.finish()

    @pl.when(row == 0)
    def _():
        copies.make(slot_low[0], low.at[upper], low_in.at[upper], across).wait_send()

    @pl.when(row == 1)
    def _():
        for k in (0, 1):
            copies.make(slot_part[k], part_t.at[k], part_in.at[k], across).wait_send()


def per_device(sources, factor, block_mask, inverse_diagonal):
    return pl.pallas_call(
        kernel,
        out_shape=jax.ShapeDtypeStruct(sources.shape, F32),
        in_specs=[
            pl.BlockSpec(memory_space=pl.ANY),
            pl.BlockSpec(memory_space=pl.ANY),
            pl.BlockSpec(memory_space=pltpu.SMEM),
            pl.BlockSpec(memory_space=pl.ANY),
        ],
        out_specs=pl.BlockSpec(memory_space=pltpu.VMEM),
        scratch_shapes=[
            pltpu.VMEM((2, HALF, SHOTS), F32),
            pltpu.VMEM((2, 16, FULL), F32),
            pltpu.VMEM((2, FULL, HALF), F32),
            pltpu.VMEM((2, 2, 16, 2, 16, HALF), F32),
            pltpu.VMEM((2, HALF, FULL), BF16),
            pltpu.VMEM((2, HALF, FULL), BF16),
            pltpu.VMEM((2, FULL, HALF), BF16),
            pltpu.VMEM((2, FULL, HALF), BF16),
            pltpu.VMEM((FULL, SHOTS), F32),
            pltpu.VMEM((FULL, SHOTS), F32),
            pltpu.VMEM((FULL, 2 * SHOTS), BF16),
            pltpu.VMEM((SHOTS, FULL), F32),
            pltpu.VMEM((2, HALF, SHOTS), F32),
            pltpu.VMEM((HALF, SHOTS), F32),
            pltpu.VMEM((FULL, SHOTS), F32),
            pltpu.VMEM((HALF, SHOTS), F32),
            pltpu.VMEM((SHOTS, HALF), F32),
            pltpu.VMEM((4, SHOTS, 256), F32),
            pltpu.VMEM((4, SHOTS, 256), F32),
            pltpu.SemaphoreType.DMA((4,)),
            pltpu.SemaphoreType.DMA((COPIES,)),
            pltpu.SemaphoreType.DMA((COPIES,)),
        ],
        compiler_params=pltpu.CompilerParams(
            collective_id=0, has_side_effects=True, vmem_limit_bytes=48 * 2**20
        ),
        cost_estimate=pl.CostEstimate(
            flops=3 * 8 * FULL * FULL * SHOTS, bytes_accessed=6 * 2**20, transcendentals=0
        ),
    )(sources, factor, block_mask, inverse_diagonal)


def solution(mesh):
    placed = (
        P("depth", None, "rows", "shots"),
        P("depth", None, ("rows", "shots"), None),
        P("depth", None, None, None),
        P("depth", None, None, "rows"),
    )
    return jax.shard_map(
        per_device,
        mesh=mesh,
        in_specs=placed,
        out_specs=P("depth", None, "rows", "shots"),
        check_vma=False,
    )
```

time: 303 us -> 82.8 us (0.27)
  waiting for transfers between devices: 258 us -> 0 us
  Pallas kernels: 0 us -> 76.4 us
  matrix products: 23.5 us -> 0 us
  between operations: 14.6 us -> 0.01 us
  local copies, waits for them, and re-layouts: 1.48 us -> 5.62 us
    all_gather x1 -> x0, waiting for transfers between devices: 137 us -> none  [per_device(): tiles = lax.all_gather(masked, 'shots', axis=1, tiled=True)]
    psum x3 -> x0, waiting for transfers between devices: 112 us -> none  [the longest x1 38.3 us: per_device(): high = lax.psum(product('rs,sn->rn', inverse_diagonal[0, 1], own), 'rows')]
    pallas_call x0 -> x1, Pallas kernels: none -> 76.4 us  [per_device(): pl.pallas_call(kernel, out_shape=jax.ShapeDtypeStruct(sources.shape, F32)...]
    dot_general x6 -> x0, matrix products: 23.4 us -> none  [product(): jnp.einsum(spec, left, right, precision=lax.Precision.HIGH, preferred_ele...]
    reduce_scatter x1 -> x0, waiting for transfers between devices: 8.44 us -> none  [per_device(): lax.psum_scatter(update, 'depth', scatter_dimension=0, tiled=True)[0]]
    unnamed x4 -> x9, local copies, waits for them, and re-layouts: 0.01 us -> 5.62 us
  transfers between devices with their start and end apart: 5 -> 0, of which waited for: 5 -> 0; matrix products, arithmetic and copies ran while one was open for 1% -> 0% of each run, Pallas kernels for 0% -> 0%
where the time goes in v2:
time: 82.8 us; the launch traced here: 82 us
  Pallas kernels  76.4 us (92%)
  local copies, waits for them, and re-layouts  5.62 us (7%)
    pallas_call x1, Pallas kernels, per_device(): pl.pallas_call(kernel, out_shape=jax.ShapeDtypeStruct(sources.shape, F32)...  76.4 us
    unnamed x9, local copies, waits for them, and re-layouts  5.62 us

profile of v2, /device:TPU:0, one launch (start us, length us, event | category | flops | bytes accessed | tf_op | source)
XLA Modules:
  0.0 82.0 jit_solution(11624759878349030344)
XLA Ops:
  0.0 0.0 copy-start
  0.0 2.2 %copy-done = f32[1,2,1024,512]{3,2,1,0:T(8,128)S(1)} copy-done((f32[1,2,1024,512]{3,2,1,0:T(8,128)S(1)}, f32[1,2,1024,512]{3,2,1,0:T(8,128)}, u32[]{:S(2)}) %copy-start) | copy-done | bytes 4194328
  2.2 0.0 copy-start.1
  2.2 1.0 %copy-done.1 = f32[1,2,512,128]{3,2,1,0:T(8,128)S(1)} copy-done((f32[1,2,512,128]{3,2,1,0:T(8,128)S(1)}, f32[1,2,512,128]{3,2,1,0:T(8,128)}, u32[]{:S(2)}) %copy-start.1) | copy-done | bytes 524312
  3.2 0.0 copy-start.2
  3.2 0.9 %copy-done.2 = f32[1,2,16,1024]{3,2,1,0:T(8,128)S(1)} copy-done((f32[1,2,16,1024]{3,2,1,0:T(8,128)S(1)}, f32[1,2,16,1024]{3,2,1,0:T(8,128)}, u32[]{:S(2)}) %copy-start.2) | copy-done | bytes 131096
  4.1 0.0 copy-start.3
  4.1 0.7 copy-done.3
  4.8 76.4 %shard_map.46 = f32[1,2,512,128]{3,2,1,0:T(8,128)S(1)} custom-call(f32[1,2,512,128]{3,2,1,0:T(8,128)S(1)} %copy-done.1, f32[1,2,16,1024]{3,2,1,0:T(8,128)S(1)} %copy-done.2, s32[1,2,8,8]{3,2,1,0:T(8,128)S(1)} %copy-done.3, f32[1,2,1024,512]{3,2,1,0:T(8,128)S(1)} %copy-done), custom_call_target="tpu_custom_call" | custom-call | flops 3221225472 | bytes 6291456 | tf_op jit(solution)/shard_map/pallas_call | solution.py:407
  81.2 0.8 copy.6
Async XLA Ops:
  0.0 2.2 %copy-start = (f32[1,2,1024,512]{3,2,1,0:T(8,128)S(1)}, f32[1,2,1024,512]{3,2,1,0:T(8,128)}, u32[]{:S(2)}) copy-start(f32[1,2,1024,512]{3,2,1,0:T(8,128)} %inv_hbm.1) | copy-start | bytes 12582916
  2.2 1.0 %copy-start.1 = (f32[1,2,512,128]{3,2,1,0:T(8,128)S(1)}, f32[1,2,512,128]{3,2,1,0:T(8,128)}, u32[]{:S(2)}) copy-start(f32[1,2,512,128]{3,2,1,0:T(8,128)} %src_hbm.1) | copy-start | bytes 1572868
  3.2 0.9 %copy-start.2 = (f32[1,2,16,1024]{3,2,1,0:T(8,128)S(1)}, f32[1,2,16,1024]{3,2,1,0:T(8,128)}, u32[]{:S(2)}) copy-start(f32[1,2,16,1024]{3,2,1,0:T(8,128)} %fac_hbm.1) | copy-start | bytes 393220
  4.1 0.7 copy-start.3

commit v3 on v2

--- a/solution.py
+++ b/solution.py
@@ -217,11 +217,6 @@
     def pair(t):
         return [(t, 0), (t, 1)]
 
-    for p in parts:
-        swap_beside(p)
-    for p in pair(0):
-        send_own(p)
-
     def invert_split(m):
         loads[2 + m].wait()
 
@@ -230,75 +225,37 @@
             rows = pl.ds(pl.multiple_of(i * 256, 256), 256)
             inv_high[m, rows], inv_low[m, rows] = split(inv[m, rows])
 
-    loads[1].wait()
-    invert_split(0)
-    for p in pair(0):
-        wait_beside(p)
-        send_side(p)
-        send_unit(p, 0)
-    source_pair = jnp.concatenate(split(src[0]), axis=1)
-
-    @pl.loop(0, 4)
-    def _(i):
-        rows = pl.ds(pl.multiple_of(i * 256, 256), 256)
-        low[rows] = wide_product(inv_high[0, rows], inv_low[0, rows], source_pair)
-
     bottom, upper = pl.ds(HALF, HALF), pl.ds(0, HALF)
-    copies.send(slot_low[1], low.at[bottom], low_in.at[bottom], across)
-
-    @pl.when(row == 0)
-    def _():
-        copies.make(slot_low[0], low.at[upper], low_in.at[upper], across).start()
-
-    for p in pair(0):
-        for s in (1, -1):
-            relay_one(p, s)
-        send_unit(p, -1)
-        send_unit(p, 1)
-    for p in pair(1):
-        send_own(p)
-        wait_beside(p)
-        send_side(p)
-        send_unit(p, 0)
-    for p in pair(0):
-        wait_far(p)
-        send_unit(p, 2)
-    invert_split(1)
-    for p in pair(0):
-        relay_two(p, 0)
-    for p in pair(1):
-        for s in (1, -1):
-            relay_one(p, s)
-        send_unit(p, -1)
-        send_unit(p, 1)
-    for p in pair(0):
-        relay_two(p, -1)
-        relay_two(p, 1)
-    for p in pair(1):
-        wait_far(p)
-        send_unit(p, 2)
-    for p in pair(0):
-        relay_two(p, 2)
-    for p in pair(1):
-        relay_two(p, 0)
-
-    copies.arrived(slot_low[1], low_in.at[bottom], across)
-
-    @pl.when(row == 1)
-    def _():
-        copies.arrived(slot_low[0], low_in.at[upper], across)
-
-    @pl.when(row == 0)
-    def _():
-        low_in[upper] = low[upper]
-
-    low_in[bottom] = low[bottom] + low_in[bottom]
-    low_pair[...] = jnp.concatenate(split(low_in[...]), axis=1)
-    low_t[...] = low_in[...].T
-
-    for p in pair(1):
-        relay_two(p, -1)
-        relay_two(p, 1)
+
+    def low_share():
+        source_pair = jnp.concatenate(split(src[0]), axis=1)
+
+        @pl.loop(0, 4)
+        def _(i):
+            rows = pl.ds(pl.multiple_of(i * 256, 256), 256)
+            low[rows] = wide_product(inv_high[0, rows], inv_low[0, rows], source_pair)
+
+    def low_send():
+        copies.send(slot_low[1], low.at[bottom], low_in.at[bottom], across)
+
+        @pl.when(row == 0)
+        def _():
+            copies.make(slot_low[0], low.at[upper], low_in.at[upper], across).start()
+
+    def low_sum():
+        copies.arrived(slot_low[1], low_in.at[bottom], across)
+
+        @pl.when(row == 1)
+        def _():
+            copies.arrived(slot_low[0], low_in.at[upper], across)
+
+        @pl.when(row == 0)
+        def _():
+            low_in[upper] = low[upper]
+
+        low_in[bottom] = low[bottom] + low_in[bottom]
+        low_pair[...] = jnp.concatenate(split(low_in[...]), axis=1)
+        low_t[...] = low_in[...].T
 
     def forward(t):
         @pl.loop(0, 4)
@@ -314,14 +271,13 @@
                 total += wide_product(high, rest, low_pair[cols])
             update[t, rows] = total
 
-    def level_one(t):
         @pl.when(core != t)
         def _():
-            copy = copies.make(slot_update, update.at[t], update_in, twin)
-            copy.start()
-            copy.wait_send()
-            copies.arrived(slot_top, top_t, twin)
-
+            copies.make(slot_update, update.at[t], update_in, twin).start()
+
+    high_copy = copies.make(slot_high, high_out.at[bottom], high_in, across)
+
+    def level_one_down(t):
         @pl.when(core == t)
         def _():
             copies.arrived(slot_update, update_in, twin)
@@ -332,39 +288,83 @@
                 rows = pl.ds(pl.multiple_of(i * 256, 256), 256)
                 high_out[rows] = wide_product(inv_high[1, rows], inv_low[1, rows], own_pair)
 
-            copy = copies.make(slot_high, high_out.at[bottom], high_in, across)
-            copy.start()
+            high_copy.start()
+
+    def level_one_up(t):
+        @pl.when(core == t)
+        def _():
             upper_pair = jnp.concatenate(split(high_out[upper].T), axis=0)
             total = tall_product(upper_pair, inv_high[1, upper], inv_low[1, upper])
-            copy.wait()
+            high_copy.wait()
             lower_pair = jnp.concatenate(split((high_out[bottom] + high_in[...]).T), axis=0)
             total += tall_product(lower_pair, inv_high[1, bottom], inv_low[1, bottom])
-            top_t[...] = total
-            copy = copies.make(slot_top, top_t, top_t, twin)
-            copy.start()
+            top_t[t] = total
+            copies.make(slot_top, top_t.at[t], top_t.at[t], twin).start()
             out_ref[0, 1] = total.T
-            copy.wait_send()
 
     def backward(t):
-        top_pair = jnp.concatenate(split(top_t[...]), axis=0)
+        @pl.when(core != t)
+        def _():
+            copies.arrived(slot_top, top_t.at[t], twin)
+
+        top_pair = jnp.concatenate(split(top_t[t]), axis=0)
         for k in range(4):
             cols = pl.ds(k * 256, 256)
             share = tall_product(top_pair, tiles_high[t, :, cols], tiles_low[t, :, cols])
             part_t[k] = share if t == 0 else part_t[k] + share
 
-    for p in pair(0):
-        for u in units:
-            wait_two_far(p, u)
-    for p in pair(1):
-        relay_two(p, 2)
-    for p in pair(1):
-        for u in units:
-            wait_two_far(p, u)
-    for t in range(2):
-        forward(t)
-    for t in range(2):
-        level_one(t)
-        backward(t)
+    def each(t, step, *rest):
+        for p in pair(t):
+            step(p, *rest)
+
+    each(0, swap_beside)
+    each(0, send_own)
+    each(1, swap_beside)
+    loads[1].wait()
+    invert_split(0)
+    low_share()
+    each(0, wait_beside)
+    each(0, send_side)
+    each(0, send_unit, 0)
+    low_send()
+    each(1, send_own)
+    each(1, wait_beside)
+    each(1, send_side)
+    for s in (1, -1):
+        each(0, relay_one, s)
+    for s in (1, -1):
+        each(0, send_unit, s)
+    each(0, relay_two, 0)
+    each(0, wait_far)
+    each(0, send_unit, 2)
+    each(1, send_unit, 0)
+    invert_split(1)
+    for s in (1, -1):
+        each(0, relay_two, s)
+    for s in (1, -1):
+        each(1, relay_one, s)
+    each(0, relay_two, 2)
+    for s in (1, -1):
+        each(1, send_unit, s)
+    each(1, relay_two, 0)
+    low_sum()
+    each(1, wait_far)
+    each(1, send_unit, 2)
+    for u in units:
+        each(0, wait_two_far, u)
+    forward(0)
+    for s in (1, -1):
+        each(1, relay_two, s)
+    level_one_down(0)
+    each(1, relay_two, 2)
+    for u in units:
+        each(1, wait_two_far, u)
+    forward(1)
+    level_one_down(1)
+    level_one_up(0)
+    backward(0)
+    level_one_up(1)
+    backward(1)
 
     for k in (2, 3):
         copies.send(slot_part[k], part_t.at[k], part_in.at[k], across)
@@ -392,6 +392,12 @@
     out_ref[0, 0] = low_in[pl.ds(0, HALF)]
 
     copies.finish()
+    for t in range(2):
+
+        @pl.when(core == t)
+        def _():
+            copies.make(slot_update, update.at[1 - t], update_in, twin).wait_send()
+            copies.make(slot_top, top_t.at[t], top_t.at[t], twin).wait_send()
 
     @pl.when(row == 0)
     def _():
@@ -408,10 +414,10 @@
         kernel,
         out_shape=jax.ShapeDtypeStruct(sources.shape, F32),
         in_specs=[
-            pl.BlockSpec(memory_space=pl.ANY),
-            pl.BlockSpec(memory_space=pl.ANY),
+            pl.BlockSpec(memory_space=pltpu.HBM),
+            pl.BlockSpec(memory_space=pltpu.HBM),
             pl.BlockSpec(memory_space=pltpu.SMEM),
-            pl.BlockSpec(memory_space=pl.ANY),
+            pl.BlockSpec(memory_space=pltpu.HBM),
         ],
         out_specs=pl.BlockSpec(memory_space=pltpu.VMEM),
         scratch_shapes=[
@@ -431,7 +437,7 @@
             pltpu.VMEM((HALF, SHOTS), F32),
             pltpu.VMEM((FULL, SHOTS), F32),
             pltpu.VMEM((HALF, SHOTS), F32),
-            pltpu.VMEM((SHOTS, HALF), F32),
+            pltpu.VMEM((2, SHOTS, HALF), F32),
             pltpu.VMEM((4, SHOTS, 256), F32),
             pltpu.VMEM((4, SHOTS, 256), F32),
             pltpu.SemaphoreType.DMA((4,)),
@@ -439,7 +445,7 @@
             pltpu.SemaphoreType.DMA((COPIES,)),
         ],
         compiler_params=pltpu.CompilerParams(
-            collective_id=0, has_side_effects=True, vmem_limit_bytes=48 * 2**20
+            collective_id=0, has_side_effects=True, vmem_limit_bytes=60 * 2**20
         ),
         cost_estimate=pl.CostEstimate(
             flops=3 * 8 * FULL * FULL * SHOTS, bytes_accessed=6 * 2**20, transcendentals=0

time: 82.8 us -> 64.6 us (0.78)
  Pallas kernels: 76.4 us -> 62.5 us
  local copies, waits for them, and re-layouts: 5.62 us -> 1.87 us
    pallas_call x1, Pallas kernels: 76.4 us -> 62.5 us  [per_device(): pl.pallas_call(kernel, out_shape=jax.ShapeDtypeStruct(sources.shape, F32)...]
    unnamed x9 -> x1, local copies, waits for them, and re-layouts: 5.62 us -> 1.87 us
where the time goes in v3:
time: 64.6 us; the launch traced here: 64.4 us
  Pallas kernels  62.5 us (97%)
  local copies, waits for them, and re-layouts  1.87 us (3%)
    pallas_call x1, Pallas kernels, per_device(): pl.pallas_call(kernel, out_shape=jax.ShapeDtypeStruct(sources.shape, F32)...  62.5 us
    unnamed x1, local copies, waits for them, and re-layouts  1.87 us

profile of v3, /device:TPU:0, one launch (start us, length us, event | category | flops | bytes accessed | tf_op | source)
XLA Modules:
  0.0 64.4 jit_solution(17696143090757528082)
XLA Ops:
  0.0 62.5 %shard_map.46 = f32[1,2,512,128]{3,2,1,0:T(8,128)} custom-call(f32[1,2,512,128]{3,2,1,0:T(8,128)} %src_hbm.1, f32[1,2,16,1024]{3,2,1,0:T(8,128)} %fac_hbm.1, s32[1,2,8,8]{3,2,1,0:T(8,128)} %mask_ref.1, f32[1,2,1024,512]{3,2,1,0:T(8,128)} %inv_hbm.1), custom_call_target="tpu_custom_call" | custom-call | flops 3221225472 | bytes 6291456 | tf_op jit(solution)/shard_map/pallas_call | solution.py:413
  62.5 1.9 %copy.6 = f32[1,2,512,128]{3,2,1,0:T(8,128)} copy(f32[1,2,512,128]{3,2,1,0:T(8,128)} %shard_map.46) | data formatting | bytes 1048576

commit v4 on v3

--- a/solution.py
+++ b/solution.py
@@ -64,7 +64,7 @@
             copy.wait_send()
 
 
-COPIES = 104
+COPIES = 112
 
 
 def kernel(
@@ -92,6 +92,8 @@
     top_t,
     part_t,
     part_in,
+    answer_t,
+    answers,
     load_sems,
     send_sems,
     recv_sems,
@@ -129,6 +131,17 @@
     for partner in partners:
         pl.semaphore_signal(barrier, inc=1, device_id=partner, device_id_type=MESH)
 
+    def invert_split(m):
+        loads[2 + m].wait()
+
+        @pl.loop(0, 4)
+        def _(i):
+            rows = pl.ds(pl.multiple_of(i * 256, 256), 256)
+            inv_high[m, rows], inv_low[m, rows] = split(inv[m, rows])
+
+    def write_out(m):
+        return pltpu.make_async_copy(answers.at[m], out_ref.at[0, m], load_sems.at[4 + m])
+
     loads[0].wait()
     row_block = row * 4 + zy // 4
     for t in range(2):
@@ -137,6 +150,7 @@
             piece = fac[t, :, k * BLOCK : (k + 1) * BLOCK] * scale
             tiles[t, k // 4, zy, xl, :, (k % 4) * BLOCK : (k % 4 + 1) * BLOCK] = piece
 
+    invert_split(0)
     pl.semaphore_wait(barrier, len(partners))
 
     copies = Copies(send_sems, recv_sems)
@@ -150,9 +164,9 @@
     slot_two = {(p, u, s): copies.slot() for p in parts for u in units for s in (1, -1)}
     slot_two_far = {(p, u, s): copies.slot() for p in parts for u in units for s in (1, -1)}
     slot_low = [copies.slot() for _ in range(2)]
-    slot_update = copies.slot()
-    slot_high = copies.slot()
-    slot_top = copies.slot()
+    slot_update = [copies.slot() for _ in range(4)]
+    slot_high = [copies.slot() for _ in range(2)]
+    slot_top = [copies.slot() for _ in range(2)]
     slot_part = [copies.slot() for _ in range(4)]
     assert copies.count <= COPIES
 
@@ -217,14 +231,6 @@
     def pair(t):
         return [(t, 0), (t, 1)]
 
-    def invert_split(m):
-        loads[2 + m].wait()
-
-        @pl.loop(0, 4)
-        def _(i):
-            rows = pl.ds(pl.multiple_of(i * 256, 256), 256)
-            inv_high[m, rows], inv_low[m, rows] = split(inv[m, rows])
-
     bottom, upper = pl.ds(HALF, HALF), pl.ds(0, HALF)
 
     def low_share():
@@ -255,12 +261,14 @@
 
         low_in[bottom] = low[bottom] + low_in[bottom]
         low_pair[...] = jnp.concatenate(split(low_in[...]), axis=1)
-        low_t[...] = low_in[...].T
-
-    def forward(t):
-        @pl.loop(0, 4)
-        def _(i):
-            rows = pl.ds(pl.multiple_of(i * 128, 128), 128)
+
+    def update_copy(t, i):
+        rows = pl.ds(i * 128, 128)
+        return copies.make(slot_update[i], update.at[t, rows], update_in.at[rows], twin)
+
+    def forward(t, chunks):
+        for i in chunks:
+            rows = pl.ds(i * 128, 128)
             total = jnp.zeros((128, SHOTS), F32)
             for h in range(2):
                 block = tiles[t, h, pl.ds(i * 4, 4)].reshape(128, HALF)
@@ -271,47 +279,73 @@
                 total += wide_product(high, rest, low_pair[cols])
             update[t, rows] = total
 
-        @pl.when(core != t)
-        def _():
-            copies.make(slot_update, update.at[t], update_in, twin).start()
-
-    high_copy = copies.make(slot_high, high_out.at[bottom], high_in, across)
+            @pl.when(core != t)
+            def _():
+                update_copy(t, i).start()
+
+    def high_copy(i):
+        rows = pl.ds(HALF + i * 256, 256)
+        return copies.make(slot_high[i], high_out.at[rows], high_in.at[pl.ds(i * 256, 256)], across)
 
     def level_one_down(t):
         @pl.when(core == t)
         def _():
-            copies.arrived(slot_update, update_in, twin)
+            for i in range(4):
+                update_copy(t, i).wait_recv()
             own_pair = jnp.concatenate(split(src[1] - update[t] - update_in[...]), axis=1)
-
-            @pl.loop(0, 4)
-            def _(i):
-                rows = pl.ds(pl.multiple_of(i * 256, 256), 256)
+            for i in (2, 3, 0, 1):
+                rows = pl.ds(i * 256, 256)
                 high_out[rows] = wide_product(inv_high[1, rows], inv_low[1, rows], own_pair)
-
-            high_copy.start()
+                if i >= 2:
+                    high_copy(i - 2).start()
+
+    def top_copy(t, i):
+        return copies.make(slot_top[i], top_t.at[t, i], top_t.at[t, i], twin)
 
     def level_one_up(t):
         @pl.when(core == t)
         def _():
             upper_pair = jnp.concatenate(split(high_out[upper].T), axis=0)
-            total = tall_product(upper_pair, inv_high[1, upper], inv_low[1, upper])
-            high_copy.wait()
+            halves = [pl.ds(i * 256, 256) for i in range(2)]
+            for i in range(2):
+                top_t[t, i] = tall_product(upper_pair, inv_high[1, upper, halves[i]], inv_low[1, upper, halves[i]])
+            for i in range(2):
+                high_copy(i).wait()
             lower_pair = jnp.concatenate(split((high_out[bottom] + high_in[...]).T), axis=0)
-            total += tall_product(lower_pair, inv_high[1, bottom], inv_low[1, bottom])
-            top_t[t] = total
-            copies.make(slot_top, top_t.at[t], top_t.at[t], twin).start()
-            out_ref[0, 1] = total.T
+            for i in range(2):
+                top_t[t, i] = top_t[t, i] + tall_product(
+                    lower_pair, inv_high[1, bottom, halves[i]], inv_low[1, bottom, halves[i]]
+                )
+                top_copy(t, i).start()
+
+    def top_out(t):
+        @pl.when(core == t)
+        def _():
+            for i in range(2):
+                answers[1, pl.ds(i * 256, 256)] = top_t[t, i].T
+            write_out(1).start()
+
+    def part_copy(k):
+        return copies.make(slot_part[k], part_t.at[k], part_in.at[k], across)
 
     def backward(t):
         @pl.when(core != t)
         def _():
-            copies.arrived(slot_top, top_t.at[t], twin)
-
-        top_pair = jnp.concatenate(split(top_t[t]), axis=0)
-        for k in range(4):
+            for i in range(2):
+                top_copy(t, i).wait_recv()
+
+        top_pair = jnp.concatenate(split(jnp.concatenate([top_t[t, 0], top_t[t, 1]], axis=1)), axis=0)
+        for k in (2, 3, 0, 1):
             cols = pl.ds(k * 256, 256)
             share = tall_product(top_pair, tiles_high[t, :, cols], tiles_low[t, :, cols])
             part_t[k] = share if t == 0 else part_t[k] + share
+            if t == 1 and k >= 2:
+                copies.send(slot_part[k], part_t.at[k], part_in.at[k], across)
+            elif t == 1:
+
+                @pl.when(row == 1)
+                def _():
+                    part_copy(k).start()
 
     def each(t, step, *rest):
         for p in pair(t):
@@ -321,7 +355,6 @@
     each(0, send_own)
     each(1, swap_beside)
     loads[1].wait()
-    invert_split(0)
     low_share()
     each(0, wait_beside)
     each(0, send_side)
@@ -352,27 +385,23 @@
     each(1, send_unit, 2)
     for u in units:
         each(0, wait_two_far, u)
-    forward(0)
-    for s in (1, -1):
-        each(1, relay_two, s)
+    forward(0, (0, 1))
+    each(1, relay_two, 1)
+    forward(0, (2, 3))
+    each(1, relay_two, -1)
     level_one_down(0)
     each(1, relay_two, 2)
     for u in units:
         each(1, wait_two_far, u)
-    forward(1)
+    forward(1, range(4))
     level_one_down(1)
     level_one_up(0)
+    top_out(0)
     backward(0)
+    low_t[...] = low_in[...].T
     level_one_up(1)
     backward(1)
-
-    for k in (2, 3):
-        copies.send(slot_part[k], part_t.at[k], part_in.at[k], across)
-
-    @pl.when(row == 1)
-    def _():
-        for k in (0, 1):
-            copies.make(slot_part[k], part_t.at[k], part_in.at[k], across).start()
+    top_out(1)
 
     def final(k):
         cols = pl.ds(k * 256, 256)
@@ -381,23 +410,25 @@
         pair_ = jnp.concatenate(split(target), axis=0)
         return tall_product(pair_, inv_high[0, cols], inv_low[0, cols])
 
-    answer = final(2) + final(3)
-    low_in[pl.ds(0, HALF)] = answer.T
+    answer_t[...] = final(2) + final(3)
 
     @pl.when(row == 0)
     def _():
-        more = final(0) + final(1)
-        low_in[pl.ds(0, HALF)] = low_in[pl.ds(0, HALF)] + more.T
-
-    out_ref[0, 0] = low_in[pl.ds(0, HALF)]
+        answer_t[...] = answer_t[...] + final(0)
+        answer_t[...] = answer_t[...] + final(1)
+
+    answers[0] = answer_t[...].T
+    write_out(0).start()
 
     copies.finish()
     for t in range(2):
 
         @pl.when(core == t)
         def _():
-            copies.make(slot_update, update.at[1 - t], update_in, twin).wait_send()
-            copies.make(slot_top, top_t.at[t], top_t.at[t], twin).wait_send()
+            for i in range(4):
+                update_copy(1 - t, i).wait_send()
+            for i in range(2):
+                top_copy(t, i).wait_send()
 
     @pl.when(row == 0)
     def _():
@@ -406,7 +437,10 @@
     @pl.when(row == 1)
     def _():
         for k in (0, 1):
-            copies.make(slot_part[k], part_t.at[k], part_in.at[k], across).wait_send()
+            part_copy(k).wait_send()
+
+    for m in range(2):
+        write_out(m).wait()
 
 
 def per_device(sources, factor, block_mask, inverse_diagonal):
@@ -419,7 +453,7 @@
             pl.BlockSpec(memory_space=pltpu.SMEM),
             pl.BlockSpec(memory_space=pltpu.HBM),
         ],
-        out_specs=pl.BlockSpec(memory_space=pltpu.VMEM),
+        out_specs=pl.BlockSpec(memory_space=pltpu.HBM),
         scratch_shapes=[
             pltpu.VMEM((2, HALF, SHOTS), F32),
             pltpu.VMEM((2, 16, FULL), F32),
@@ -437,10 +471,12 @@
             pltpu.VMEM((HALF, SHOTS), F32),
             pltpu.VMEM((FULL, SHOTS), F32),
             pltpu.VMEM((HALF, SHOTS), F32),
-            pltpu.VMEM((2, SHOTS, HALF), F32),
+            pltpu.VMEM((2, 2, SHOTS, 256), F32),
             pltpu.VMEM((4, SHOTS, 256), F32),
             pltpu.VMEM((4, SHOTS, 256), F32),
-            pltpu.SemaphoreType.DMA((4,)),
+            pltpu.VMEM((SHOTS, HALF), F32),
+            pltpu.VMEM((2, HALF, SHOTS), F32),
+            pltpu.SemaphoreType.DMA((6,)),
             pltpu.SemaphoreType.DMA((COPIES,)),
             pltpu.SemaphoreType.DMA((COPIES,)),
         ],

time: 64.6 us -> 63.6 us (0.985)
  Pallas kernels: 62.5 us -> 61.5 us
    pallas_call x1, Pallas kernels: 62.5 us -> 61.5 us  [per_device(): pl.pallas_call(kernel, out_shape=jax.ShapeDtypeStruct(sources.shape, F32)...]
where the time goes in v4:
time: 63.6 us; the launch traced here: 63.4 us
  Pallas kernels  61.5 us (97%)
  local copies, waits for them, and re-layouts  1.87 us (3%)
    pallas_call x1, Pallas kernels, per_device(): pl.pallas_call(kernel, out_shape=jax.ShapeDtypeStruct(sources.shape, F32)...  61.5 us
    unnamed x1, local copies, waits for them, and re-layouts  1.87 us

profile of v4, /device:TPU:0, one launch (start us, length us, event | category | flops | bytes accessed | tf_op | source)
XLA Modules:
  0.0 63.4 jit_solution(7550571218248091260)
XLA Ops:
  0.0 61.5 %shard_map.46 = f32[1,2,512,128]{3,2,1,0:T(8,128)} custom-call(f32[1,2,512,128]{3,2,1,0:T(8,128)} %src_hbm.1, f32[1,2,16,1024]{3,2,1,0:T(8,128)} %fac_hbm.1, s32[1,2,8,8]{3,2,1,0:T(8,128)} %mask_ref.1, f32[1,2,1024,512]{3,2,1,0:T(8,128)} %inv_hbm.1), custom_call_target="tpu_custom_call" | custom-call | flops 3221225472 | bytes 6291456 | tf_op jit(solution)/shard_map/pallas_call | solution.py:447
  61.5 1.9 %copy.6 = f32[1,2,512,128]{3,2,1,0:T(8,128)} copy(f32[1,2,512,128]{3,2,1,0:T(8,128)} %shard_map.46) | data formatting | bytes 1048576

commit v5 on v4

--- a/solution.py
+++ b/solution.py
@@ -9,6 +9,7 @@
 F32 = jnp.float32
 BF16 = jnp.bfloat16
 BLOCK = 128
+DIRECT = (0, 1)
 HALF = 512
 FULL = 1024
 SHOTS = 128
@@ -127,7 +128,7 @@
         load.start()
 
     barrier = pltpu.get_barrier_semaphore()
-    partners = [neighbour(a, s) for a in (0, 1) for s in (1, -1)] + [beside, across, twin]
+    partners = [neighbour(a, s) for a in (0, 1) for s in (1, -1)] + [beside, across, twin, neighbour(0, 2), neighbour(1, 2)]
     for partner in partners:
         pl.semaphore_signal(barrier, inc=1, device_id=partner, device_id_type=MESH)
 
@@ -183,6 +184,8 @@
         piece = tiles.at[t, h, zy, xl]
         for s in (1, -1):
             copies.send(slot_own[p, s], piece, piece, neighbour(first[h], s))
+        if t in DIRECT:
+            copies.send(slot_far[p, 1], piece, piece, neighbour(first[h], 2))
 
     def wait_beside(p):
         t, h = p
@@ -193,37 +196,50 @@
         piece = tiles.at[t, h, zy, 1 - xl]
         for s in (1, -1):
             copies.send(slot_side[p, s], piece, piece, neighbour(first[h], s))
+        if t in DIRECT:
+            copies.send(slot_far[p, -1], piece, piece, neighbour(first[h], 2))
 
     def send_unit(p, u):
         t, h = p
         piece = tiles.at[t, h, unit_place(h, u, 0)]
         for s in (1, -1):
             copies.send(slot_two[p, u, s], piece, piece, neighbour(1 - first[h], s))
+        if t == 1 and u == 2:
+            copies.send(slot_two_far[p, u, 1], piece, piece, neighbour(1 - first[h], 2))
 
     def relay_one(p, s):
         t, h = p
         where = unit_place(h, -s, 0)
         copies.arrived(slot_own[p, s], tiles.at[t, h, where, xl], neighbour(first[h], -s))
         copies.arrived(slot_side[p, s], tiles.at[t, h, where, 1 - xl], neighbour(first[h], -s))
-        piece = tiles.at[t, h, where, 0 if s == 1 else 1]
-        copies.send(slot_far[p, s], piece, piece, neighbour(first[h], s))
+        if t not in DIRECT:
+            piece = tiles.at[t, h, where, 0 if s == 1 else 1]
+            copies.send(slot_far[p, s], piece, piece, neighbour(first[h], s))
 
     def wait_far(p):
         t, h = p
         for s in (1, -1):
-            piece = tiles.at[t, h, unit_place(h, 2, 0), 0 if s == 1 else 1]
-            copies.arrived(slot_far[p, s], piece, neighbour(first[h], -s))
+            which = 0 if s == 1 else 1
+            if t in DIRECT:
+                which = xl if s == 1 else 1 - xl
+            piece = tiles.at[t, h, unit_place(h, 2, 0), which]
+            copies.arrived(slot_far[p, s], piece, neighbour(first[h], 2))
 
     def relay_two(p, u):
         t, h = p
         for s in (1, -1):
             where = unit_place(h, u, -s)
             copies.arrived(slot_two[p, u, s], tiles.at[t, h, where], neighbour(1 - first[h], -s))
+            if t == 1 and u == 2:
+                continue
             piece = tiles.at[t, h, where, 0 if s == 1 else 1]
             copies.send(slot_two_far[p, u, s], piece, piece, neighbour(1 - first[h], s))
 
     def wait_two_far(p, u):
         t, h = p
+        if t == 1 and u == 2:
+            copies.arrived(slot_two_far[p, u, 1], tiles.at[t, h, unit_place(h, u, 2)], neighbour(1 - first[h], 2))
+            return
         for s in (1, -1):
             piece = tiles.at[t, h, unit_place(h, u, 2), 0 if s == 1 else 1]
             copies.arrived(slot_two_far[p, u, s], piece, neighbour(1 - first[h], -s))
@@ -354,13 +370,13 @@
     each(0, swap_beside)
     each(0, send_own)
     each(1, swap_beside)
+    each(1, send_own)
     loads[1].wait()
     low_share()
     each(0, wait_beside)
     each(0, send_side)
     each(0, send_unit, 0)
     low_send()
-    each(1, send_own)
     each(1, wait_beside)
     each(1, send_side)
     for s in (1, -1):

time: 63.6 us -> 61.7 us (0.970)
  Pallas kernels: 61.5 us -> 59.6 us
    pallas_call x1, Pallas kernels: 61.5 us -> 59.6 us  [per_device(): pl.pallas_call(kernel, out_shape=jax.ShapeDtypeStruct(sources.shape, F32)...]
where the time goes in v5:
time: 61.7 us; the launch traced here: 61.5 us
  Pallas kernels  59.6 us (97%)
  local copies, waits for them, and re-layouts  1.87 us (3%)
    pallas_call x1, Pallas kernels, per_device(): pl.pallas_call(kernel, out_shape=jax.ShapeDtypeStruct(sources.shape, F32)...  59.6 us
    unnamed x1, local copies, waits for them, and re-layouts  1.87 us

profile of v5, /device:TPU:0, one launch (start us, length us, event | category | flops | bytes accessed | tf_op | source)
XLA Modules:
  0.0 61.5 jit_solution(12365977590629091061)
XLA Ops:
  0.0 59.6 %shard_map.46 = f32[1,2,512,128]{3,2,1,0:T(8,128)} custom-call(f32[1,2,512,128]{3,2,1,0:T(8,128)} %src_hbm.1, f32[1,2,16,1024]{3,2,1,0:T(8,128)} %fac_hbm.1, s32[1,2,8,8]{3,2,1,0:T(8,128)} %mask_ref.1, f32[1,2,1024,512]{3,2,1,0:T(8,128)} %inv_hbm.1), custom_call_target="tpu_custom_call" | custom-call | flops 3221225472 | bytes 6291456 | tf_op jit(solution)/shard_map/pallas_call | solution.py:463
  59.7 1.9 %copy.6 = f32[1,2,512,128]{3,2,1,0:T(8,128)} copy(f32[1,2,512,128]{3,2,1,0:T(8,128)} %shard_map.46) | data formatting | bytes 1048576

commit v6 on v5

--- a/solution.py
+++ b/solution.py
@@ -278,16 +278,22 @@
         low_in[bottom] = low[bottom] + low_in[bottom]
         low_pair[...] = jnp.concatenate(split(low_in[...]), axis=1)
 
+    def layer(i):
+        return (z + i) % 4
+
+    def layer_rows(i):
+        return pl.ds(pl.multiple_of(layer(i) * 128, 128), 128)
+
     def update_copy(t, i):
-        rows = pl.ds(i * 128, 128)
+        rows = layer_rows(i)
         return copies.make(slot_update[i], update.at[t, rows], update_in.at[rows], twin)
 
     def forward(t, chunks):
         for i in chunks:
-            rows = pl.ds(i * 128, 128)
+            rows = layer_rows(i)
             total = jnp.zeros((128, SHOTS), F32)
             for h in range(2):
-                block = tiles[t, h, pl.ds(i * 4, 4)].reshape(128, HALF)
+                block = tiles[t, h, pl.ds(layer(i) * 4, 4)].reshape(128, HALF)
                 high, rest = split(block)
                 cols = pl.ds(h * HALF, HALF)
                 tiles_high[t, rows, cols] = high
@@ -406,10 +412,14 @@
     forward(0, (2, 3))
     each(1, relay_two, -1)
     level_one_down(0)
+    each(1, wait_two_far, 0)
+    forward(1, (0,))
     each(1, relay_two, 2)
-    for u in units:
-        each(1, wait_two_far, u)
-    forward(1, range(4))
+    each(1, wait_two_far, 1)
+    each(1, wait_two_far, -1)
+    forward(1, (1, 3))
+    each(1, wait_two_far, 2)
+    forward(1, (2,))
     level_one_down(1)
     level_one_up(0)
     top_out(0)

time: 61.7 us -> 61.4 us (level)
  no operation moved by 1% of the time
where the time goes in v6:
time: 61.4 us; the launch traced here: 61.2 us
  Pallas kernels  59.3 us (97%)
  local copies, waits for them, and re-layouts  1.87 us (3%)
    pallas_call x1, Pallas kernels, per_device(): pl.pallas_call(kernel, out_shape=jax.ShapeDtypeStruct(sources.shape, F32)...  59.3 us
    unnamed x1, local copies, waits for them, and re-layouts  1.87 us

profile of v6, /device:TPU:0, one launch (start us, length us, event | category | flops | bytes accessed | tf_op | source)
XLA Modules:
  0.0 61.2 jit_solution(15716517634188696392)
XLA Ops:
  0.0 59.3 %shard_map.46 = f32[1,2,512,128]{3,2,1,0:T(8,128)} custom-call(f32[1,2,512,128]{3,2,1,0:T(8,128)} %src_hbm.1, f32[1,2,16,1024]{3,2,1,0:T(8,128)} %fac_hbm.1, s32[1,2,8,8]{3,2,1,0:T(8,128)} %mask_ref.1, f32[1,2,1024,512]{3,2,1,0:T(8,128)} %inv_hbm.1), custom_call_target="tpu_custom_call" | custom-call | flops 3221225472 | bytes 6291456 | tf_op jit(solution)/shard_map/pallas_call | solution.py:473
  59.3 1.9 %copy.6 = f32[1,2,512,128]{3,2,1,0:T(8,128)} copy(f32[1,2,512,128]{3,2,1,0:T(8,128)} %shard_map.46) | data formatting | bytes 1048576

commit v7 on v6

--- a/solution.py
+++ b/solution.py
@@ -331,14 +331,17 @@
             halves = [pl.ds(i * 256, 256) for i in range(2)]
             for i in range(2):
                 top_t[t, i] = tall_product(upper_pair, inv_high[1, upper, halves[i]], inv_low[1, upper, halves[i]])
-            for i in range(2):
-                high_copy(i).wait()
-            lower_pair = jnp.concatenate(split((high_out[bottom] + high_in[...]).T), axis=0)
-            for i in range(2):
-                top_t[t, i] = top_t[t, i] + tall_product(
-                    lower_pair, inv_high[1, bottom, halves[i]], inv_low[1, bottom, halves[i]]
-                )
-                top_copy(t, i).start()
+            for c in range(2):
+                high_copy(c).wait()
+                rows = pl.ds(HALF + c * 256, 256)
+                lower = (high_out[rows] + high_in[pl.ds(c * 256, 256)]).T
+                lower_pair = jnp.concatenate(split(lower), axis=0)
+                for i in range(2):
+                    top_t[t, i] = top_t[t, i] + tall_product(
+                        lower_pair, inv_high[1, rows, halves[i]], inv_low[1, rows, halves[i]]
+                    )
+                    if c == 1:
+                        top_copy(t, i).start()
 
     def top_out(t):
         @pl.when(core == t)

time: 61.4 us -> 61.2 us (level)
  no operation moved by 1% of the time
where the time goes in v7:
time: 61.2 us; the launch traced here: 61 us
  Pallas kernels  59.1 us (97%)
  local copies, waits for them, and re-layouts  1.87 us (3%)
    pallas_call x1, Pallas kernels, per_device(): pl.pallas_call(kernel, out_shape=jax.ShapeDtypeStruct(sources.shape, F32)...  59.1 us
    unnamed x1, local copies, waits for them, and re-layouts  1.87 us

profile of v7, /device:TPU:0, one launch (start us, length us, event | category | flops | bytes accessed | tf_op | source)
XLA Modules:
  0.0 61.0 jit_solution(17914582206172967347)
XLA Ops:
  0.0 59.1 %shard_map.46 = f32[1,2,512,128]{3,2,1,0:T(8,128)} custom-call(f32[1,2,512,128]{3,2,1,0:T(8,128)} %src_hbm.1, f32[1,2,16,1024]{3,2,1,0:T(8,128)} %fac_hbm.1, s32[1,2,8,8]{3,2,1,0:T(8,128)} %mask_ref.1, f32[1,2,1024,512]{3,2,1,0:T(8,128)} %inv_hbm.1), custom_call_target="tpu_custom_call" | custom-call | flops 3221225472 | bytes 6291456 | tf_op jit(solution)/shard_map/pallas_call | solution.py:476
  59.1 1.9 %copy.6 = f32[1,2,512,128]{3,2,1,0:T(8,128)} copy(f32[1,2,512,128]{3,2,1,0:T(8,128)} %shard_map.46) | data formatting | bytes 1048576
